TPU v7x, 256 devices: a whole 4x4x8 slice. The times are simulated.
256 devices in a mesh: rows: 128 (over y, z, x), rep: 2 (over core).
Axes of the slice: x: 4, y: 4, z: 8, core: 2. Of those that a mesh axis runs over, the one named last changes fastest.
Arguments:
- features: bfloat16 [131072, 128], P('rows'), may hold values from -6 to 6
- weight: bfloat16 [128, 256], replicated, may hold values from -0.5 to 0.5
- tiles: bfloat16 [1024, 64, 128, 128], P('rows', 'rep'), may hold values from -0.0625 to 0.0625
- tile_cols: int32 [1024, 64], P('rows', 'rep'), may hold values from 0 to 1023, as said below
- order: int32 [1024], replicated, may hold values from 0 to 1023, as said below
- cotangent: bfloat16 [131072, 256], P('rows'), may hold values from -24 to 24
Outputs:
- activated: bfloat16 [131072, 256], P('rows')
- feature_grad: float32 [131072, 128], P('rows')
- weight_grad: float32 [128, 256], replicated
Inputs may be any that keep to these rules, and one draw needn't show every extreme that they name: `tile_cols`: the 64 column tiles of one tile row are all different. Among the 32 slots of the 8 tile rows that one index of rows and one index of rep hold, exactly 2 name (through order) blocks owned by each index of rows, that is blocks o * 8 to (o + 1) * 8 - 1 for index o; all blocks named by the slots of one index of rows are different. `order`: A permutation of the tile rows.
All inputs are finite; a program needn't handle non-finite values.
Results may differ from a plain program's by a relative error of at most 0.0055.
Values may be sent and summed in bfloat16 or wider, within the bound.
No kernel may reach another device: no remote copies, remote signals or barrier semaphores. Data moves between devices by JAX's collectives and lax.ppermute only.
A program may use at most 192 MiB of HBM per device.

v0:
```python
import jax
import jax.numpy as jnp
from jax import lax
from jax.sharding import PartitionSpec as P


def body(features, weight, tiles, tile_cols, order, cotangent):
    tile_rows = tiles.shape[0]
    row_slots = tiles.shape[1]
    side = tiles.shape[2]
    width = features.shape[1]
    n_tiles = order.shape[0]
    senders = lax.axis_size("rows")
    copies = lax.axis_size("rep")
    core = lax.axis_index("rep")
    slots = tile_rows * row_slots
    per_owner = slots // senders
    own_rows = features.shape[0]
    half = own_rows // copies
    offset = core * half
    labels = jnp.arange(n_tiles, dtype=jnp.int32)
    flat_cols = tile_cols.reshape(-1)
    block = jnp.sum(jnp.where(flat_cols[:, None] == labels[None, :], order[None, :], 0), axis=1)
    owner = block // tile_rows
    local_block = block % tile_rows
    owner_hits = (owner[:, None] == jnp.arange(senders, dtype=jnp.int32)[None, :]).astype(jnp.int32)
    before = jnp.cumsum(owner_hits, axis=0) - owner_hits
    rank = jnp.sum(before * owner_hits, axis=1)
    position = owner * per_owner + rank
    slot_ids = jnp.arange(slots, dtype=jnp.int32)
    match = position[None, :] == slot_ids[:, None]
    wanted = jnp.sum(jnp.where(match, local_block[None, :], 0), axis=1)
    slot_of = jnp.sum(jnp.where(match, slot_ids[None, :], 0), axis=1)
    incoming = lax.all_to_all(
        wanted.reshape(senders, per_owner), "rows", split_axis=0, concat_axis=0, tiled=True
    )
    feature_blocks = features.reshape(tile_rows, side, width)
    replies = feature_blocks[incoming]
    arrived = lax.all_to_all(replies, "rows", split_axis=0, concat_axis=0, tiled=True).reshape(
        slots, side, width
    )
    picked = arrived[position].reshape(tile_rows, row_slots, side, width)
    local_sum = jnp.einsum("bkij,bkjf->bif", tiles, picked, preferred_element_type=jnp.float32)
    summed = lax.psum(local_sum.reshape(own_rows, width), "rep")
    aggregated = summed.astype(jnp.bfloat16)
    pre = jnp.dot(aggregated, weight, preferred_element_type=jnp.float32)
    sig = jax.nn.sigmoid(pre)
    activated = (pre * sig).astype(jnp.bfloat16)
    pre_grad = (cotangent.astype(jnp.float32) * sig * (1.0 + pre * (1.0 - sig))).astype(
        jnp.bfloat16
    )
    agg_half = lax.dynamic_slice_in_dim(aggregated, offset, half, 0)
    grad_half = lax.dynamic_slice_in_dim(pre_grad, offset, half, 0)
    local_weight = jnp.dot(agg_half.T, grad_half, preferred_element_type=jnp.float32)
    weight_grad = lax.psum(local_weight, ("rows", "rep"))
    spread = jnp.dot(pre_grad, weight.T, preferred_element_type=jnp.float32).astype(jnp.bfloat16)
    spread_blocks = spread.reshape(tile_rows, side, width)
    terms = jnp.einsum("bkij,bif->bkjf", tiles, spread_blocks, preferred_element_type=jnp.float32)
    outgoing = terms.reshape(slots, side, width)[slot_of]
    targets = jnp.arange(tile_rows, dtype=jnp.int32)
    received = lax.all_to_all(
        outgoing.reshape(senders, per_owner, side, width),
        "rows",
        split_axis=0,
        concat_axis=0,
        tiled=True,
    )
    selector = (incoming.reshape(-1)[None, :] == targets[:, None]).astype(jnp.float32)
    owned = jnp.dot(
        selector, received.reshape(slots, side * width), precision=lax.Precision.HIGHEST
    )
    feature_grad = lax.psum(owned.reshape(own_rows, width), "rep")
    return (activated, feature_grad, weight_grad)


def solution(mesh):
    in_specs = (
        P("rows", None),
        P(),
        P("rows", "rep", None, None),
        P("rows", "rep"),
        P(),
        P("rows", None),
    )
    out_specs = (P("rows", None), P("rows", None), P())
    return jax.shard_map(body, mesh=mesh, in_specs=in_specs, out_specs=out_specs, check_vma=False)
```

profile of v0, /device:TPU:1, one launch (start us, length us, event | category | flops | bytes accessed | tf_op | source)
XLA Modules:
  0.0 762.0 jit_solution(630971453472746934)
XLA Ops:
  7.2 0.0 copy-start
  7.2 0.8 eq.66
  8.0 1.0 select_reduce_fusion
  9.0 0.1 copy.19
  9.1 0.2 fusion.5
  9.4 0.2 fusion.7
  9.6 0.2 select_reduce_fusion.1
  9.8 0.1 all_to_all.14
  9.9 26.7 %all_to_all.22 = s32[128,1,2]{2,1,0:T(1,128)S(1)} all-to-all(s32[128,1,2]{2,1,0:T(1,128)S(1)} %bitcast.72), channel_id=1, replica_groups=mesh['rows'=128,'rep'=2] {'rows'}, dimensions={0} | all-to-all | bytes 2048 | tf_op jit(solution)/shard_map/all_to_all | solution.py:34
  36.6 0.1 reshape.215
  36.8 0.0 copy-done
  36.8 8.6 %gather_fusion = bf16[256,128,128]{2,1,0:T(8,128)(2,1)} fusion(bf16[8,128,128]{2,1,0:T(8,128)(2,1)S(1)} %bitcast.62, s32[1024]{0:T(1024)S(1)} %pad_clamp_fusion.2), kind=kCustom, calls=%fused_computation | custom fusion | bytes 16778240 | tf_op jit(solution)/shard_map/gather | solution.py:38
  45.4 7.7 %all-to-all-start.1 = ((bf16[128,2,128,128]{3,2,1,0:T(8,128)(2,1)}), bf16[128,2,128,128]{3,2,1,0:T(8,128)(2,1)}, u32[]{:S(2)}, u32[]{:S(2)}) async-start(bf16[128,2,128,128]{3,2,1,0:T(8,128)(2,1)} %bitcast.65), calls=%async_computation.1 | async-start | bytes 16777216 | tf_op jit(solution)/shard_map/all_to_all | solution.py:39
  53.1 183.2 %all-to-all-done.1 = bf16[128,2,128,128]{3,2,1,0:T(8,128)(2,1)} async-done(((bf16[128,2,128,128]{3,2,1,0:T(8,128)(2,1)}), bf16[128,2,128,128]{3,2,1,0:T(8,128)(2,1)}, u32[]{:S(2)}, u32[]{:S(2)}) %all-to-all-start.1) | async-done | bytes 8388640 | tf_op jit(solution)/shard_map/all_to_all | solution.py:39
  236.3 12.0 %gather_fusion.1 = bf16[256,128,128]{2,1,0:T(8,128)(2,1)} fusion(bf16[256,128,128]{2,1,0:T(8,128)(2,1)} %bitcast.8, s32[1024]{0:T(1024)S(1)} %pad_clamp_fusion.1), kind=kCustom, calls=%fused_computation.1 | custom fusion | bytes 16778240 | tf_op jit(solution)/shard_map/gather | solution.py:42
  248.3 0.0 copy-start.2
  248.3 0.0 copy-start.3
  248.3 8.2 %fusion.14 = f32[8,128,128,1]{1,2,3,0:T(8,128)S(1)} fusion(bf16[8,32,128,128]{3,2,1,0:T(8,128)(2,1)} %param.8, bf16[8,32,128,128]{3,2,1,0:T(8,128)(2,1)} %bitcast.66), kind=kOutput, calls=%fused_computation.55 | convolution fusion | flops 1073741824 | bytes 17301504 | tf_op jit(solution)/shard_map/bkij,bkjf->bif/dot_general | solution.py:43
  256.5 8.9 %all-reduce.7 = bf16[1024,128]{1,0:T(8,128)(2,1)S(1)} all-reduce(f32[1024,128]{1,0:T(8,128)S(1)} %bitcast.67), channel_id=1, replica_groups=mesh['rows'=128,'rep'=2] {'rep'}, use_global_device_ids=true, to_apply=%region_5.6 | all-reduce | flops 131072 | bytes 786432 | tf_op jit(solution)/shard_map/psum | solution.py:44
  265.4 0.0 copy-done.2
  265.4 0.0 copy-done.3
  265.4 1.4 multiply_convert_fusion
  266.9 0.3 convolution_convert_fusion
  267.1 11.5 %fusion.13 = f32[8,128,32,128]{3,1,2,0:T(8,128)} fusion(bf16[8,128,128,1]{2,1,3,0:T(8,128)(2,1)S(1)} %bitcast.68, bf16[8,32,128,128]{3,2,1,0:T(8,128)(2,1)} %param.8), kind=kOutput, calls=%fused_computation.54 | convolution fusion | flops 1073741824 | bytes 25427968 | tf_op jit(solution)/shard_map/bkij,bif->bkjf/dot_general | solution.py:58
  278.6 17.7 %gather_fusion.2 = f32[256,128,128]{1,2,0:T(8,128)} fusion(f32[256,128,128]{1,2,0:T(8,128)} %bitcast.63, s32[1024]{0:T(1024)S(1)} %pad_clamp_fusion), kind=kCustom, calls=%fused_computation.2 | custom fusion | bytes 33555456 | tf_op jit(solution)/shard_map/gather | solution.py:59
  296.3 17.5 %copy.23 = f32[256,128,128]{2,1,0:T(8,128)} copy(f32[256,128,128]{1,2,0:T(8,128)} %gather_fusion.2) | data formatting | bytes 33554432 | tf_op jit(solution)/shard_map/gather | solution.py:59
  313.7 7.8 %all-to-all-start.2 = ((f32[128,2,128,128]{3,2,1,0:T(8,128)}), f32[128,2,128,128]{3,2,1,0:T(8,128)}, u32[]{:S(2)}, u32[]{:S(2)}) async-start(f32[128,2,128,128]{3,2,1,0:T(8,128)} %bitcast.64), calls=%async_computation.2 | async-start | bytes 33554432 | tf_op jit(solution)/shard_map/all_to_all | solution.py:61
  321.5 0.0 all-reduce.6.cloned.1.call-start
  321.6 0.5 broadcast.254
  322.1 0.8 reduce.3
  322.9 0.1 eq.79
  323.1 0.9 fusion.3
  324.0 0.0 all-reduce.6.cloned.1.call-update
  324.0 0.0 all-reduce.4.cloned.1.call-start
  324.0 365.4 %all-to-all-done.2 = f32[128,2,128,128]{3,2,1,0:T(8,128)} async-done(((f32[128,2,128,128]{3,2,1,0:T(8,128)}), f32[128,2,128,128]{3,2,1,0:T(8,128)}, u32[]{:S(2)}, u32[]{:S(2)}) %all-to-all-start.2) | async-done | bytes 16777248 | tf_op jit(solution)/shard_map/all_to_all | solution.py:61
  689.4 0.0 copy-start.1
  689.4 19.9 %fusion = f32[8,16384]{1,0:T(8,128)S(1)} fusion(f32[32,8,128,128]{3,2,1,0:T(8,128)} %bitcast.33, s32[256]{0:T(256)S(1)} %eq.79), kind=kOutput, calls=%fused_computation.3 | convolution fusion | flops 402655232 | bytes 17302528 | tf_op jit(solution)/shard_map/dot_general | solution.py:69
  709.3 0.9 reshape.212
  710.2 0.0 all-reduce.4.cloned.1.call-update
  710.2 0.0 all-reduce.6.cloned.1.call-done
  710.2 41.5 %all-reduce.4.cloned.1.call-done = f32[1024,128]{1,0:T(8,128)} async-done(((f32[1024,128]{1,0:T(8,128)}), f32[1024,128]{1,0:T(8,128)}) %all-reduce.4.cloned.1.call-update) | async-done | bytes 524304 | tf_op jit(solution)/shard_map/psum | solution.py:72
  751.7 1.9 copy.37
  753.6 1.6 copy.38
  755.2 0.0 copy-done.1
  (15 shorter events, 0.2 us)
Async XLA Ops:
  7.2 29.6 %copy-start = (bf16[1024,128]{1,0:T(8,128)(2,1)S(1)}, bf16[1024,128]{1,0:T(8,128)(2,1)}, u32[]{:S(2)}) copy-start(bf16[1024,128]{1,0:T(8,128)(2,1)} %param.6) | copy-start | bytes 786436
  45.4 191.0 %all-to-all-start.1 = ((bf16[128,2,128,128]{3,2,1,0:T(8,128)(2,1)}), bf16[128,2,128,128]{3,2,1,0:T(8,128)(2,1)}, u32[]{:S(2)}, u32[]{:S(2)}) async-start(bf16[128,2,128,128]{3,2,1,0:T(8,128)(2,1)} %bitcast.65), calls=%async_computation.1 | async-start | bytes 16777216 | tf_op jit(solution)/shard_map/all_to_all | solution.py:39
  248.3 17.1 %copy-start.2 = (bf16[128,256]{1,0:T(8,128)(2,1)S(1)}, bf16[128,256]{1,0:T(8,128)(2,1)}, u32[]{:S(2)}) copy-start(bf16[128,256]{1,0:T(8,128)(2,1)} %param.7) | copy-start | bytes 196612
  248.3 17.1 %copy-start.3 = (bf16[1024,256]{1,0:T(8,128)(2,1)S(1)}, bf16[1024,256]{1,0:T(8,128)(2,1)}, u32[]{:S(2)}) copy-start(bf16[1024,256]{1,0:T(8,128)(2,1)} %param.11) | copy-start | bytes 1572868
  313.7 375.6 %all-to-all-start.2 = ((f32[128,2,128,128]{3,2,1,0:T(8,128)}), f32[128,2,128,128]{3,2,1,0:T(8,128)}, u32[]{:S(2)}, u32[]{:S(2)}) async-start(f32[128,2,128,128]{3,2,1,0:T(8,128)} %bitcast.64), calls=%async_computation.2 | async-start | bytes 33554432 | tf_op jit(solution)/shard_map/all_to_all | solution.py:61
  321.5 388.7 %all-reduce.6.cloned.1.call-start = ((), (), s32[]{:S(2)}) async-start(), calls=%async_computation.4 | async-start | bytes 262144 | tf_op jit(solution)/shard_map/psum | solution.py:55
  324.0 427.8 %all-reduce.4.cloned.1.call-start = ((), (), s32[]{:S(2)}) async-start(), calls=%async_computation.3 | async-start | bytes 1048576 | tf_op jit(solution)/shard_map/psum | solution.py:72
  689.4 65.8 %copy-start.1 = (bf16[1024,128]{1,0:T(8,128)(2,1)S(1)}, bf16[1024,128]{1,0:T(8,128)(2,1)}, u32[]{:S(2)}) copy-start(bf16[1024,128]{1,0:T(8,128)(2,1)} %param.6) | copy-start | bytes 786436
Sparse Core Ops, SparseCore 0:
  328.5 370.8 all-reduce.5
  710.3 41.3 all-reduce.3
where the time goes:
time: 763 us; the launch traced here: 762 us
  waiting for transfers between devices  590 us (77%)
  local copies, waits for them, and re-layouts  61.9 us (8%)
  matrix products  42.1 us (6%)
  blocking collectives  35.6 us (5%)
  starting transfers between devices  15.5 us (2%)
  between operations  14.2 us (2%)
    all_to_all x1, waiting for transfers between devices, body(): lax.all_to_all(outgoing.reshape(senders, per_owner, side, width), 'rows',...  365 us
    all_to_all x1, waiting for transfers between devices, body(): lax.all_to_all(replies, 'rows', split_axis=0, concat_axis=0, tiled=True)  183 us
    psum x1, waiting for transfers between devices, body(): feature_grad = lax.psum(owned.reshape(own_rows, width), 'rep')  41.5 us
    gather x2, local copies, waits for them, and re-layouts, body(): outgoing = terms.reshape(slots, side, width)[slot_of]  35.1 us
    all_to_all x1, blocking collectives, body(): lax.all_to_all(wanted.reshape(senders, per_owner), 'rows', split_axis=0,...  26.7 us
    dot_general x1, matrix products, body(): jnp.dot(selector, received.reshape(slots, side * width), precision=lax.Pr...  19.9 us
  transfers between devices with their start and end apart: 4, of which 3 were waited for; matrix products, arithmetic and copies ran while one was open for 3% of the time, Pallas kernels for 0%

commit v1 on v0

v1 whole, which is shorter than its diff:
```python
import functools

import jax
import jax.numpy as jnp
from jax import lax
from jax.experimental import pallas as pl
from jax.experimental.pallas import tpu as pltpu
from jax.sharding import PartitionSpec as P

BF = jnp.bfloat16
F32 = jnp.float32
BOTH = ("rows", "rep")
SWAP = ((0, 1), (1, 0))


def torus(n_rows):
    return {128: (4, 8, 4), 8: (2, 2, 2)}[n_rows]


def ring(n_rows, axis):
    sizes = torus(n_rows)
    pairs = []
    for i in range(n_rows):
        c = [i // (sizes[1] * sizes[2]), i // sizes[2] % sizes[1], i % sizes[2]]
        for core in range(2):
            t = list(c)
            t[axis] = (t[axis] + (1 if core == 0 else -1)) % sizes[axis]
            pairs.append((2 * i + core, 2 * ((t[0] * sizes[1] + t[1]) * sizes[2] + t[2]) + core))
    return tuple(pairs)


PARTS = ((0, 2, (2, 0, 1)), (2, 3, (0, 1, 2)), (5, 3, (1, 2, 0)))


def gather_parts(n_rows, own):
    sizes = torus(n_rows)
    out = []
    for first, count, axes in PARTS:
        held = own[first : first + count]
        for axis in axes:
            pieces = [held]
            for _ in range(sizes[axis] - 1):
                pieces.append(lax.ppermute(pieces[-1], BOTH, ring(n_rows, axis)))
            if axis == axes[-1]:
                out.extend(pieces)
            else:
                held = jnp.concatenate(pieces, 0)
    return jnp.concatenate(out, 0)


def scatter_parts(n_rows, terms):
    sizes = torus(n_rows)
    out = []
    for first, count, axes in PARTS:
        held = terms[first * n_rows : (first + count) * n_rows]
        for axis in axes[::-1]:
            n = sizes[axis]
            size = held.shape[0] // n
            total = held[(n - 1) * size :]
            for d in range(n - 2, -1, -1):
                came = lax.ppermute(total, BOTH, ring(n_rows, axis))
                total = came.astype(F32) + held[d * size : (d + 1) * size].astype(F32)
                if d > 0 or axis != axes[0]:
                    total = total.astype(BF)
            held = total
        out.append(held)
    return jnp.concatenate(out, 0)


def positions(n_rows, tile_rows, block, here, core, sign):
    sizes = torus(n_rows)
    owner, local = block // tile_rows, block % tile_rows

    def split(i):
        return (i // (sizes[1] * sizes[2]), i // sizes[2] % sizes[1], i % sizes[2])

    turn = jnp.where(core == 0, sign, -sign)
    mine, theirs = split(here), split(owner)
    offset = [(turn * (mine[a] - theirs[a]) + sizes[a]) % sizes[a] for a in range(3)]
    place = jnp.zeros_like(block)
    for first, count, axes in PARTS:
        a, b, c = axes
        at = ((offset[c] * sizes[b] + offset[b]) * sizes[a] + offset[a]) * count + local - first
        place = jnp.where((local >= first) & (local < first + count), first * n_rows + at, place)
    return place


def pack_kernel(width, core_ref, tiles_ref, own_ref, send_ref, zero_ref):
    side = tiles_ref.shape[2]
    half = side // 2
    zero_ref[...] = jnp.zeros_like(zero_ref)

    def fill(first, second):
        for q in range(tiles_ref.shape[1] // width):
            group = [tiles_ref[0, q * width + i] for i in range(width)]
            first[0, q] = jnp.concatenate([t[:, :half] for t in group], 1)
            second[0, q] = jnp.concatenate([t[:, half:] for t in group], 1)

    @pl.when(core_ref[0] == 0)
    def _():
        fill(own_ref, send_ref)

    @pl.when(core_ref[0] != 0)
    def _():
        fill(send_ref, own_ref)


def pack(core, tiles, n_tiles, width):
    rows, slots, side, _ = tiles.shape
    packed = jax.ShapeDtypeStruct((rows, slots // width, side, width * side // 2), BF)
    spec = pl.BlockSpec((1, slots // width, side, width * side // 2), lambda b: (b, 0, 0, 0))
    zeros = jax.ShapeDtypeStruct((n_tiles, side // 2, side), BF)
    return pl.pallas_call(
        functools.partial(pack_kernel, width),
        grid=(rows,),
        in_specs=[
            pl.BlockSpec(memory_space=pltpu.SMEM),
            pl.BlockSpec((1, slots, side, side), lambda b: (b, 0, 0, 0)),
        ],
        out_specs=[
            spec,
            spec,
            pl.BlockSpec((n_tiles // rows, side // 2, side), lambda b: (b, 0, 0)),
        ],
        out_shape=[packed, packed, zeros],
        compiler_params=pltpu.CompilerParams(vmem_limit_bytes=40 * 2**20),
        cost_estimate=pl.CostEstimate(flops=0, bytes_accessed=33 * 2**20, transcendentals=0),
        name="pack_tiles",
    )(core, tiles)


def forward_kernel(place_ref, own_ref, other_ref, blocks_ref, sum_ref, held, sems):
    b = pl.program_id(0)
    rows = pl.num_programs(0)
    slots = held.shape[1]
    half = held.shape[2]

    def fetch(row):
        slot = lax.rem(row, 2)

        @pl.loop(0, slots, unroll=8)
        def _(k):
            at = place_ref[row * slots + k]
            pltpu.make_async_copy(blocks_ref.at[at], held.at[slot, k], sems.at[slot]).start()

    @pl.when(b == 0)
    def _():
        fetch(b)

    @pl.when(b + 1 < rows)
    def _():
        fetch(b + 1)

    now = lax.rem(b, 2)
    pltpu.make_async_copy(blocks_ref.at[pl.ds(0, slots)], held.at[now], sems.at[now]).wait()
    total = jnp.zeros(sum_ref.shape[1:], F32)
    width = own_ref.shape[3] // half
    k = 0
    for ref in (own_ref, other_ref):
        for q in range(ref.shape[1]):
            right = held[now, k : k + width].reshape(width * half, -1)
            total += jnp.dot(ref[0, q], right, preferred_element_type=F32)
            k += width
    sum_ref[0] = total


def forward(place, own, other, blocks):
    rows, groups, side, wide = own.shape
    slots = place.shape[0] // rows
    spec = pl.BlockSpec((1, groups, side, wide), lambda b: (b, 0, 0, 0))
    return pl.pallas_call(
        forward_kernel,
        grid=(rows,),
        in_specs=[
            pl.BlockSpec(memory_space=pltpu.SMEM),
            spec,
            spec,
            pl.BlockSpec(memory_space=pl.ANY),
        ],
        out_specs=pl.BlockSpec((1, side, blocks.shape[2]), lambda b: (b, 0, 0)),
        out_shape=jax.ShapeDtypeStruct((rows, side, blocks.shape[2]), F32),
        scratch_shapes=[
            pltpu.VMEM((2, slots) + blocks.shape[1:], BF),
            pltpu.SemaphoreType.DMA((2,)),
        ],
        compiler_params=pltpu.CompilerParams(vmem_limit_bytes=40 * 2**20),
        cost_estimate=pl.CostEstimate(flops=2**30, bytes_accessed=2**24, transcendentals=0),
        name="forward_tiles",
    )(place, own, other, blocks)


def backward_kernel(
    core_ref, place_ref, mine_ref, came_ref, weight_ref, cot_ref, own_ref, other_ref, zero_ref,
    act_ref, terms_ref, wgrad_ref, held, sems,
):
    b = pl.program_id(0)
    rows = pl.num_programs(0)
    slots = held.shape[1]
    half = held.shape[2]
    now = lax.rem(b, 2)

    def drain(slot):
        pltpu.make_async_copy(held.at[slot], terms_ref.at[pl.ds(0, slots)], sems.at[slot]).wait()

    agg = (mine_ref[0] + came_ref[0]).astype(BF)
    weight = weight_ref[...]
    pre = jnp.dot(agg, weight, preferred_element_type=F32)
    sig = jax.nn.sigmoid(pre)
    act_ref[0] = (pre * sig).astype(BF)
    grad = (cot_ref[0].astype(F32) * sig * (1.0 + pre * (1.0 - sig))).astype(BF)
    spread = lax.dot_general(
        grad, weight, (((1,), (1,)), ((), ())), preferred_element_type=F32
    ).astype(BF)
    hid = grad.shape[1] // 2
    part = jnp.where(core_ref[0] == 0, grad[:, :hid].astype(F32), grad[:, hid:].astype(F32)).astype(BF)
    wgrad = lax.dot_general(agg, part, (((0,), (0,)), ((), ())), preferred_element_type=F32)

    @pl.when(b == 0)
    def _():
        wgrad_ref[...] = wgrad

    @pl.when(b > 0)
    def _():
        wgrad_ref[...] += wgrad

    @pl.when(b >= 2)
    def _():
        drain(now)

    width = own_ref.shape[3] // half
    k = 0
    for ref in (own_ref, other_ref):
        for q in range(ref.shape[1]):
            term = lax.dot_general(
                ref[0, q], spread, (((0,), (0,)), ((), ())), preferred_element_type=F32
            ).astype(BF)
            held[now, k : k + width] = term.reshape(width, half, -1)
            k += width

    @pl.loop(0, slots, unroll=8)
    def _(k):
        at = place_ref[b * slots + k]
        pltpu.make_async_copy(held.at[now, k], terms_ref.at[at], sems.at[now]).start()

    @pl.when(b == rows - 1)
    def _():
        drain(lax.rem(b + 1, 2))
        drain(now)


def backward(core, place, mine, came, weight, cotangent, own, other, zeros):
    rows, groups, side, wide = own.shape
    slots = place.shape[0] // rows
    feat, hid = weight.shape
    tile_spec = pl.BlockSpec((1, groups, side, wide), lambda b: (b, 0, 0, 0))
    row_spec = pl.BlockSpec((1, side, feat), lambda b: (b, 0, 0))
    hid_spec = pl.BlockSpec((1, side, hid), lambda b: (b, 0, 0))
    smem = pl.BlockSpec(memory_space=pltpu.SMEM)
    return pl.pallas_call(
        backward_kernel,
        grid=(rows,),
        in_specs=[
            smem,
            smem,
            row_spec,
            row_spec,
            pl.BlockSpec((feat, hid), lambda b: (0, 0)),
            hid_spec,
            tile_spec,
            tile_spec,
            pl.BlockSpec(memory_space=pl.ANY),
        ],
        out_specs=[
            hid_spec,
            pl.BlockSpec(memory_space=pl.ANY),
            pl.BlockSpec((feat, hid // 2), lambda b: (0, 0)),
        ],
        out_shape=[
            jax.ShapeDtypeStruct((rows, side, hid), BF),
            jax.ShapeDtypeStruct(zeros.shape, BF),
            jax.ShapeDtypeStruct((feat, hid // 2), F32),
        ],
        scratch_shapes=[
            pltpu.VMEM((2, slots) + zeros.shape[1:], BF),
            pltpu.SemaphoreType.DMA((2,)),
        ],
        input_output_aliases={8: 1},
        compiler_params=pltpu.CompilerParams(vmem_limit_bytes=40 * 2**20),
        cost_estimate=pl.CostEstimate(flops=2**30, bytes_accessed=2**24, transcendentals=2**18),
        name="backward_tiles",
    )(core, place, mine, came, weight, cotangent, own, other, zeros)


def body(features, weight, tiles, tile_cols, order, cotangent):
    tile_rows, row_slots, side, _ = tiles.shape
    width = features.shape[1]
    n_tiles = order.shape[0]
    n_rows = lax.axis_size("rows")
    here = lax.axis_index("rows")
    core = lax.axis_index("rep")
    core_ref = core.reshape(1).astype(jnp.int32)
    half = side // 2
    group = 4 if row_slots % 4 == 0 else 2

    halves = features.reshape(tile_rows, 2, half, width)
    own_half = jnp.where(core == 0, halves[:, 0], halves[:, 1])
    gathered = gather_parts(n_rows, own_half)

    own, send, zeros = pack(core_ref, tiles, n_tiles, group)
    other = lax.ppermute(send, "rep", SWAP)

    labels = jnp.arange(n_tiles, dtype=jnp.int32)
    flat = tile_cols.reshape(-1)
    block = jnp.sum(jnp.where(flat[:, None] == labels[None, :], order[None, :], 0), axis=1)
    block = block.reshape(tile_rows, row_slots)
    block = jnp.concatenate([block, lax.ppermute(block, "rep", SWAP)], 1).reshape(-1)
    gather_place = positions(n_rows, tile_rows, block, here, core, 1)
    scatter_place = positions(n_rows, tile_rows, block, here, core, -1)

    mine = forward(gather_place, own, other, gathered)
    came = lax.ppermute(mine, "rep", SWAP)
    activated, terms, wgrad = backward(
        core_ref, scatter_place, mine, came, weight,
        cotangent.reshape(tile_rows, side, -1), own, other, zeros,
    )

    bit = 1
    while bit < n_rows:
        wgrad = wgrad + lax.ppermute(wgrad, "rows", tuple((i, i ^ bit) for i in range(n_rows)))
        bit *= 2
    wother = lax.ppermute(wgrad, "rep", SWAP)
    weight_grad = jnp.where(
        core == 0, jnp.concatenate([wgrad, wother], 1), jnp.concatenate([wother, wgrad], 1)
    )

    owned = scatter_parts(n_rows, terms)
    pair = lax.ppermute(owned, "rep", SWAP)
    feature_grad = jnp.where(
        core == 0, jnp.stack([owned, pair], 1), jnp.stack([pair, owned], 1)
    ).reshape(tile_rows * side, width)
    return activated.reshape(tile_rows * side, -1), feature_grad, weight_grad


def solution(mesh):
    in_specs = (
        P("rows", None),
        P(),
        P("rows", "rep", None, None),
        P("rows", "rep"),
        P(),
        P("rows", None),
    )
    out_specs = (P("rows", None), P("rows", None), P())
    return jax.shard_map(body, mesh=mesh, in_specs=in_specs, out_specs=out_specs, check_vma=False)
```

time: 763 us -> 563 us (0.74); the launches traced: 762 us -> 554 us
  waiting for transfers between devices: 590 us -> 236 us
  starting transfers between devices: 15.5 us -> 240 us
  matrix products: 42.1 us -> 0 us
  local copies, waits for them, and re-layouts: 61.9 us -> 20.7 us
  blocking collectives: 35.6 us -> 0 us
  Pallas kernels: 0 us -> 33.5 us
  other arithmetic: 2.43 us -> 22 us
  between operations: 14.2 us -> 1.71 us
    all_to_all x2 -> x0, waiting for transfers between devices: 549 us -> none  [the longest x1 365 us: body(): lax.all_to_all(outgoing.reshape(senders, per_owner, side, width), 'rows',...]
    ppermute x0 -> x90, starting transfers between devices: none -> 240 us  [the longest x39 95.5 us: gather_parts(): pieces.append(lax.ppermute(pieces[-1], BOTH, ring(n_rows, axis)))]
    ppermute x0 -> x90, waiting for transfers between devices: none -> 236 us  [the longest x39 154 us: gather_parts(): pieces.append(lax.ppermute(pieces[-1], BOTH, ring(n_rows, axis)))]
    gather x4 -> x0, local copies, waits for them, and re-layouts: 55.7 us -> none  [the longest x2 35.1 us: body(): outgoing = terms.reshape(slots, side, width)[slot_of]]
    dot_general x6 -> x0, matrix products: 42.1 us -> none  [the longest x1 19.9 us: body(): jnp.dot(selector, received.reshape(slots, side * width), precision=lax.Pr...]
    psum x2 -> x0, waiting for transfers between devices: 41.5 us -> none  [the longest x1 41.5 us: body(): feature_grad = lax.psum(owned.reshape(own_rows, width), 'rep')]
    pallas_call x0 -> x3, Pallas kernels: none -> 33.5 us  [the longest x1 12.9 us: pack(): pl.pallas_call(functools.partial(pack_kernel, width), grid=(rows,), in_sp...]
    all_to_all x1 -> x0, blocking collectives: 26.7 us -> none  [body(): lax.all_to_all(wanted.reshape(senders, per_owner), 'rows', split_axis=0,...]
  transfers between devices with their start and end apart: 4 -> 90, of which waited for: 3 -> 61; matrix products, arithmetic and copies ran while one was open for 3% -> 5% of each run, Pallas kernels for 0% -> 2%
where the time goes in v1:
time: 563 us; the launch traced here: 554 us
  starting transfers between devices  240 us (43%)
  waiting for transfers between devices  236 us (42%)
  Pallas kernels  33.5 us (6%)
  other arithmetic  22 us (4%)
  local copies, waits for them, and re-layouts  20.7 us (4%)
    ppermute x39, waiting for transfers between devices, gather_parts(): pieces.append(lax.ppermute(pieces[-1], BOTH, ring(n_rows, axis)))  154 us
    ppermute x39, starting transfers between devices, gather_parts(): pieces.append(lax.ppermute(pieces[-1], BOTH, ring(n_rows, axis)))  95.5 us
    ppermute x39, starting transfers between devices, scatter_parts(): came = lax.ppermute(total, BOTH, ring(n_rows, axis))  66.1 us
    ppermute x39, waiting for transfers between devices, scatter_parts(): came = lax.ppermute(total, BOTH, ring(n_rows, axis))  48.5 us
    ppermute x1, starting transfers between devices, body(): other = lax.ppermute(send, 'rep', SWAP)  33 us
    ppermute x7, waiting for transfers between devices, body(): lax.ppermute(wgrad, 'rows', tuple(((i, i ^ bit) for i in range(n_rows))))  29.9 us
    ppermute x1, starting transfers between devices, body(): pair = lax.ppermute(owned, 'rep', SWAP)  26.3 us
    convert_element_type x33, other arithmetic, scatter_parts(): total = total.astype(BF)  19.6 us
  transfers between devices with their start and end apart: 90, of which 61 were waited for; matrix products, arithmetic and copies ran while one was open for 5% of the time, Pallas kernels for 2%

profile of v1, /device:TPU:1, one launch (start us, length us, event | category | flops | bytes accessed | tf_op | source)
XLA Modules:
  0.0 553.7 jit_solution(11294419258378032450)
XLA Ops:
  1.6 3.4 collective-permute-start.2
  28.9 5.7 %collective-permute-start.8 = (bf16[32,64,128]{2,1,0:T(8,128)(2,1)S(1)}, bf16[32,64,128]{2,1,0:T(8,128)(2,1)S(1)}, u32[]{:S(2)}, u32[]{:S(2)}) collective-permute-start(bf16[32,64,128]{2,1,0:T(8,128)(2,1)S(1)} %get-tuple-element.54), channel_id=1, source_target_pairs={{0,8},{1,57},{2,10},{3,59},{4,12},{5,61},{6,14},{7,63},{8,16},{9,1... | collective-permute-start | bytes 1572872 | tf_op jit(solution)/shard_map/ppermute | solution.py:43
  34.6 6.1 %collective-permute-done.8 = bf16[32,64,128]{2,1,0:T(8,128)(2,1)S(1)} collective-permute-done((bf16[32,64,128]{2,1,0:T(8,128)(2,1)S(1)}, bf16[32,64,128]{2,1,0:T(8,128)(2,1)S(1)}, u32[]{:S(2)}, u32[]{:S(2)}) %collective-permute-start.8) | collective-permute-done | bytes 524320 | tf_op jit(solution)/shard_map/ppermute | solution.py:43
  43.8 6.1 %collective-permute-done.9 = bf16[32,64,128]{2,1,0:T(8,128)(2,1)S(1)} collective-permute-done((bf16[32,64,128]{2,1,0:T(8,128)(2,1)S(1)}, bf16[32,64,128]{2,1,0:T(8,128)(2,1)S(1)}, u32[]{:S(2)}, u32[]{:S(2)}) %collective-permute-start.9) | collective-permute-done | bytes 524320 | tf_op jit(solution)/shard_map/ppermute | solution.py:43
  53.1 6.1 %collective-permute-done.10 = bf16[32,64,128]{2,1,0:T(8,128)(2,1)S(1)} collective-permute-done((bf16[32,64,128]{2,1,0:T(8,128)(2,1)S(1)}, bf16[32,64,128]{2,1,0:T(8,128)(2,1)S(1)}, u32[]{:S(2)}, u32[]{:S(2)}) %collective-permute-start.10) | collective-permute-done | bytes 524320 | tf_op jit(solution)/shard_map/ppermute | solution.py:43
  66.6 3.3 collective-permute-start.16
  75.5 4.7 collective-permute-done.18
  81.3 6.3 %collective-permute-done.19 = bf16[12,64,128]{2,1,0:T(8,128)(2,1)S(1)} collective-permute-done((bf16[12,64,128]{2,1,0:T(8,128)(2,1)S(1)}, bf16[12,64,128]{2,1,0:T(8,128)(2,1)S(1)}, u32[]{:S(2)}, u32[]{:S(2)}) %collective-permute-start.19) | collective-permute-done | bytes 196640 | tf_op jit(solution)/shard_map/ppermute | solution.py:43
  88.8 3.6 collective-permute-done.20
  100.3 4.6 collective-permute-done.22
  114.1 7.9 %collective-permute-done.14 = bf16[32,64,128]{2,1,0:T(8,128)(2,1)S(1)} collective-permute-done((bf16[32,64,128]{2,1,0:T(8,128)(2,1)S(1)}, bf16[32,64,128]{2,1,0:T(8,128)(2,1)S(1)}, u32[]{:S(2)}, u32[]{:S(2)}) %collective-permute-start.14) | collective-permute-done | bytes 524320 | tf_op jit(solution)/shard_map/ppermute | solution.py:43
  126.0 17.4 %collective-permute-done.25 = bf16[96,64,128]{2,1,0:T(8,128)(2,1)S(1)} collective-permute-done((bf16[96,64,128]{2,1,0:T(8,128)(2,1)S(1)}, bf16[96,64,128]{2,1,0:T(8,128)(2,1)S(1)}, u32[]{:S(2)}, u32[]{:S(2)}) %collective-permute-start.25) | collective-permute-done | bytes 1572896 | tf_op jit(solution)/shard_map/ppermute | solution.py:43
  146.5 17.4 %collective-permute-done.26 = bf16[96,64,128]{2,1,0:T(8,128)(2,1)S(1)} collective-permute-done((bf16[96,64,128]{2,1,0:T(8,128)(2,1)S(1)}, bf16[96,64,128]{2,1,0:T(8,128)(2,1)S(1)}, u32[]{:S(2)}, u32[]{:S(2)}) %collective-permute-start.26) | collective-permute-done | bytes 1572896 | tf_op jit(solution)/shard_map/ppermute | solution.py:43
  171.3 3.3 collective-permute-start.29
  175.7 3.3 collective-permute-start.30
  180.2 3.3 collective-permute-start.31
  184.6 3.4 collective-permute-start.32
  189.2 3.3 collective-permute-start.33
  193.6 3.3 collective-permute-start.34
  198.2 6.9 %collective-permute-done.35 = bf16[24,64,128]{2,1,0:T(8,128)(2,1)S(1)} collective-permute-done((bf16[24,64,128]{2,1,0:T(8,128)(2,1)S(1)}, bf16[24,64,128]{2,1,0:T(8,128)(2,1)S(1)}, u32[]{:S(2)}, u32[]{:S(2)}) %collective-permute-start.35) | collective-permute-done | bytes 393248 | tf_op jit(solution)/shard_map/ppermute | solution.py:43
  206.1 5.7 %collective-permute-done.36 = bf16[24,64,128]{2,1,0:T(8,128)(2,1)S(1)} collective-permute-done((bf16[24,64,128]{2,1,0:T(8,128)(2,1)S(1)}, bf16[24,64,128]{2,1,0:T(8,128)(2,1)S(1)}, u32[]{:S(2)}, u32[]{:S(2)}) %collective-permute-start.36) | collective-permute-done | bytes 393248 | tf_op jit(solution)/shard_map/ppermute | solution.py:43
  214.4 4.3 collective-permute-done.37
  224.7 12.9 %pack_tiles.1 = (bf16[8,8,128,256]{3,2,1,0:T(8,128)(2,1)S(1)}, bf16[8,8,128,256]{3,2,1,0:T(8,128)(2,1)}, bf16[1024,64,128]{2,1,0:T(8,128)(2,1)}) custom-call(s32[1]{0:T(128)} %bitcast.core_ref, bf16[8,32,128,128]{3,2,1,0:T(8,128)(2,1)} %tiles_ref.1), custom_call_target="tpu_custom_call" | custom-call | bytes 34603008 | tf_op jit(solution)/shard_map/pack_tiles/pallas_call | solution.py:113
  239.7 33.0 %collective-permute-start.1 = (bf16[8,8,128,256]{3,2,1,0:T(8,128)(2,1)}, bf16[8,8,128,256]{3,2,1,0:T(8,128)(2,1)}, u32[]{:S(2)}, u32[]{:S(2)}) collective-permute-start(bf16[8,8,128,256]{3,2,1,0:T(8,128)(2,1)} %get-tuple-element.10), channel_id=1, source_target_pairs={{0,1},{1,0},{2,3},{3,2},{4,5},{5,4},{6,7},{7,6},{8,9},{9,8},{10,11... | collective-permute-start | bytes 12582920 | tf_op jit(solution)/shard_map/ppermute | solution.py:310
  272.7 19.6 %collective-permute-done.39 = bf16[96,64,128]{2,1,0:T(8,128)(2,1)S(1)} collective-permute-done((bf16[96,64,128]{2,1,0:T(8,128)(2,1)S(1)}, bf16[96,64,128]{2,1,0:T(8,128)(2,1)S(1)}, u32[]{:S(2)}, u32[]{:S(2)}) %collective-permute-start.39) | collective-permute-done | bytes 1572896 | tf_op jit(solution)/shard_map/ppermute | solution.py:43
  299.4 12.6 %collective-permute-done.40 = bf16[96,64,128]{2,1,0:T(8,128)(2,1)} collective-permute-done((bf16[96,64,128]{2,1,0:T(8,128)(2,1)S(1)}, bf16[96,64,128]{2,1,0:T(8,128)(2,1)}, u32[]{:S(2)}, u32[]{:S(2)}) %collective-permute-start.40) | collective-permute-done | bytes 1572896 | tf_op jit(solution)/shard_map/ppermute | solution.py:43
  314.6 9.1 %forward_tiles.1.mine_ref = f32[8,128,128]{2,1,0:T(8,128)S(1)} custom-call(s32[512]{0:T(512)S(1)} %get-tuple-element.15.place_ref, bf16[8,8,128,256]{3,2,1,0:T(8,128)(2,1)S(1)} %copy-done.1, bf16[8,8,128,256]{3,2,1,0:T(8,128)(2,1)} %collective-permute-done.1.other_ref, bf16[1024,64,128]{2,1,0:T(8,128)(2,1)} %constant_dynamic-update-slice_fusion.37.blocks_ref), custom_call_target="tpu_custom_call" | custom-call | flops 1073741824 | bytes 16777216 | tf_op jit(solution)/shard_map/forward_tiles/pallas_call | solution.py:171
  323.8 5.4 collective-permute-start.41
  332.9 11.4 %backward_tiles.1 = (bf16[8,128,256]{2,1,0:T(8,128)(2,1)}, bf16[1024,64,128]{2,1,0:T(8,128)(2,1)}, f32[128,128]{1,0:T(8,128)S(1)}) custom-call(s32[1]{0:T(128)} %bitcast.core_ref, s32[512]{0:T(512)S(1)} %select_select_fusion.1.place_ref, f32[8,128,128]{2,1,0:T(8,128)S(1)} %forward_tiles.1.mine_ref, ...), custom_call_target="tpu_custom_call", output_to_operand_aliasing={{1}: (8, {})} | custom-call | flops 1073741824 | bytes 16777216 | tf_op jit(solution)/shard_map/backward_tiles/pallas_call | solution.py:259
  345.5 8.3 %collective-permute-done.42 = bf16[32,64,128]{2,1,0:T(8,128)(2,1)S(1)} collective-permute-done((bf16[32,64,128]{2,1,0:T(8,128)(2,1)S(1)}, bf16[32,64,128]{2,1,0:T(8,128)(2,1)S(1)}, u32[]{:S(2)}, u32[]{:S(2)}) %collective-permute-start.42) | collective-permute-done | bytes 524320 | tf_op jit(solution)/shard_map/ppermute | solution.py:61
  356.0 7.4 %collective-permute-done.43 = bf16[32,64,128]{2,1,0:T(8,128)(2,1)S(1)} collective-permute-done((bf16[32,64,128]{2,1,0:T(8,128)(2,1)S(1)}, bf16[32,64,128]{2,1,0:T(8,128)(2,1)S(1)}, u32[]{:S(2)}, u32[]{:S(2)}) %collective-permute-start.43) | collective-permute-done | bytes 524320 | tf_op jit(solution)/shard_map/ppermute | solution.py:61
  369.4 3.4 collective-permute-done.44
  377.1 6.1 %collective-permute-done.45 = bf16[32,64,128]{2,1,0:T(8,128)(2,1)S(1)} collective-permute-done((bf16[32,64,128]{2,1,0:T(8,128)(2,1)S(1)}, bf16[32,64,128]{2,1,0:T(8,128)(2,1)S(1)}, u32[]{:S(2)}, u32[]{:S(2)}) %collective-permute-start.45) | collective-permute-done | bytes 524320 | tf_op jit(solution)/shard_map/ppermute | solution.py:61
  384.5 3.5 collective-permute-start.46
  388.9 3.3 add_convert_fusion.5
  398.5 6.1 %collective-permute-done.47 = bf16[32,64,128]{2,1,0:T(8,128)(2,1)S(1)} collective-permute-done((bf16[32,64,128]{2,1,0:T(8,128)(2,1)S(1)}, bf16[32,64,128]{2,1,0:T(8,128)(2,1)S(1)}, u32[]{:S(2)}, u32[]{:S(2)}) %collective-permute-start.47) | collective-permute-done | bytes 524320 | tf_op jit(solution)/shard_map/ppermute | solution.py:61
  405.9 3.9 collective-permute-start.48
  413.0 3.3 add_convert_fusion.4
  420.7 16.7 %collective-permute-done.82 = f32[128,128]{1,0:T(8,128)S(1)} collective-permute-done((f32[128,128]{1,0:T(8,128)S(1)}, f32[128,128]{1,0:T(8,128)S(1)}, u32[]{:S(2)}, u32[]{:S(2)}) %collective-permute-start.82) | collective-permute-done | bytes 65568 | tf_op jit(solution)/shard_map/ppermute | solution.py:329
  451.3 4.4 collective-permute-start.86
  458.7 3.4 add_convert_fusion.3
  462.5 3.7 collective-permute-start.71
  471.1 3.2 collective-permute-start.72
  479.1 3.2 collective-permute-start.73
  490.2 3.2 collective-permute-start.75
  498.6 3.5 collective-permute-start.64
  518.5 26.3 %collective-permute-start.81 = (f32[8,64,128]{2,1,0:T(8,128)S(1)}, f32[8,64,128]{2,1,0:T(8,128)S(1)}, u32[]{:S(2)}, u32[]{:S(2)}) collective-permute-start(f32[8,64,128]{2,1,0:T(8,128)S(1)} %get-tuple-element.32), channel_id=1, source_target_pairs={{0,1},{1,0},{2,3},{3,2},{4,5},{5,4},{6,7},{7,6},{8,9},{9,8},{10,11... | collective-permute-start | bytes 786440 | tf_op jit(solution)/shard_map/ppermute | solution.py:337
  546.5 3.6 collective-permute-done.88
  (260 shorter events, 202.3 us)
Async XLA Ops:
  28.9 11.8 %collective-permute-start.8 = (bf16[32,64,128]{2,1,0:T(8,128)(2,1)S(1)}, bf16[32,64,128]{2,1,0:T(8,128)(2,1)S(1)}, u32[]{:S(2)}, u32[]{:S(2)}) collective-permute-start(bf16[32,64,128]{2,1,0:T(8,128)(2,1)S(1)} %get-tuple-element.54), channel_id=1, source_target_pairs={{0,8},{1,57},{2,10},{3,59},{4,12},{5,61},{6,14},{7,63},{8,16},{9,1... | collective-permute-start | bytes 1572872 | tf_op jit(solution)/shard_map/ppermute | solution.py:43
  40.7 9.2 %collective-permute-start.9 = (bf16[32,64,128]{2,1,0:T(8,128)(2,1)S(1)}, bf16[32,64,128]{2,1,0:T(8,128)(2,1)S(1)}, u32[]{:S(2)}, u32[]{:S(2)}) collective-permute-start(bf16[32,64,128]{2,1,0:T(8,128)(2,1)S(1)} %collective-permute-done.8), channel_id=1, source_target_pairs={{0,8},{1,57},{2,10},{3,59},{4,12},{5,61},{6,14},{7,63},{8,16},{9,1... | collective-permute-start | bytes 1572872 | tf_op jit(solution)/shard_map/ppermute | solution.py:43
  49.9 9.2 %collective-permute-start.10 = (bf16[32,64,128]{2,1,0:T(8,128)(2,1)S(1)}, bf16[32,64,128]{2,1,0:T(8,128)(2,1)S(1)}, u32[]{:S(2)}, u32[]{:S(2)}) collective-permute-start(bf16[32,64,128]{2,1,0:T(8,128)(2,1)S(1)} %collective-permute-done.9), channel_id=1, source_target_pairs={{0,8},{1,57},{2,10},{3,59},{4,12},{5,61},{6,14},{7,63},{8,16},{9,1... | collective-permute-start | bytes 1572872 | tf_op jit(solution)/shard_map/ppermute | solution.py:43
  59.2 16.2 %collective-permute-start.11 = (bf16[32,64,128]{2,1,0:T(8,128)(2,1)S(1)}, bf16[32,64,128]{2,1,0:T(8,128)(2,1)S(1)}, u32[]{:S(2)}, u32[]{:S(2)}) collective-permute-start(bf16[32,64,128]{2,1,0:T(8,128)(2,1)S(1)} %collective-permute-done.10), channel_id=1, source_target_pairs={{0,8},{1,57},{2,10},{3,59},{4,12},{5,61},{6,14},{7,63},{8,16},{9,1... | collective-permute-start | bytes 1572872 | tf_op jit(solution)/shard_map/ppermute | solution.py:43
  75.4 19.2 %collective-permute-start.12 = (bf16[32,64,128]{2,1,0:T(8,128)(2,1)S(1)}, bf16[32,64,128]{2,1,0:T(8,128)(2,1)S(1)}, u32[]{:S(2)}, u32[]{:S(2)}) collective-permute-start(bf16[32,64,128]{2,1,0:T(8,128)(2,1)S(1)} %collective-permute-done.11), channel_id=1, source_target_pairs={{0,8},{1,57},{2,10},{3,59},{4,12},{5,61},{6,14},{7,63},{8,16},{9,1... | collective-permute-start | bytes 1572872 | tf_op jit(solution)/shard_map/ppermute | solution.py:43
  80.2 7.4 %collective-permute-start.19 = (bf16[12,64,128]{2,1,0:T(8,128)(2,1)S(1)}, bf16[12,64,128]{2,1,0:T(8,128)(2,1)S(1)}, u32[]{:S(2)}, u32[]{:S(2)}) collective-permute-start(bf16[12,64,128]{2,1,0:T(8,128)(2,1)S(1)} %collective-permute-done.18), channel_id=1, source_target_pairs={{0,8},{1,57},{2,10},{3,59},{4,12},{5,61},{6,14},{7,63},{8,16},{9,1... | collective-permute-start | bytes 589832 | tf_op jit(solution)/shard_map/ppermute | solution.py:43
  94.5 19.2 %collective-permute-start.13 = (bf16[32,64,128]{2,1,0:T(8,128)(2,1)S(1)}, bf16[32,64,128]{2,1,0:T(8,128)(2,1)S(1)}, u32[]{:S(2)}, u32[]{:S(2)}) collective-permute-start(bf16[32,64,128]{2,1,0:T(8,128)(2,1)S(1)} %collective-permute-done.12), channel_id=1, source_target_pairs={{0,8},{1,57},{2,10},{3,59},{4,12},{5,61},{6,14},{7,63},{8,16},{9,1... | collective-permute-start | bytes 1572872 | tf_op jit(solution)/shard_map/ppermute | solution.py:43
  97.2 7.7 %collective-permute-start.22 = (bf16[12,64,128]{2,1,0:T(8,128)(2,1)S(1)}, bf16[12,64,128]{2,1,0:T(8,128)(2,1)S(1)}, u32[]{:S(2)}, u32[]{:S(2)}) collective-permute-start(bf16[12,64,128]{2,1,0:T(8,128)(2,1)S(1)} %collective-permute-done.21), channel_id=1, source_target_pairs={{0,8},{1,57},{2,10},{3,59},{4,12},{5,61},{6,14},{7,63},{8,16},{9,1... | collective-permute-start | bytes 589832 | tf_op jit(solution)/shard_map/ppermute | solution.py:43
  110.6 12.3 %collective-permute-start.24 = (bf16[12,64,128]{2,1,0:T(8,128)(2,1)S(1)}, bf16[12,64,128]{2,1,0:T(8,128)(2,1)S(1)}, u32[]{:S(2)}, u32[]{:S(2)}) collective-permute-start(bf16[12,64,128]{2,1,0:T(8,128)(2,1)S(1)} %collective-permute-done.23), channel_id=1, source_target_pairs={{0,8},{1,57},{2,10},{3,59},{4,12},{5,61},{6,14},{7,63},{8,16},{9,1... | collective-permute-start | bytes 589832 | tf_op jit(solution)/shard_map/ppermute | solution.py:43
  113.7 8.3 %collective-permute-start.14 = (bf16[32,64,128]{2,1,0:T(8,128)(2,1)S(1)}, bf16[32,64,128]{2,1,0:T(8,128)(2,1)S(1)}, u32[]{:S(2)}, u32[]{:S(2)}) collective-permute-start(bf16[32,64,128]{2,1,0:T(8,128)(2,1)S(1)} %collective-permute-done.13), channel_id=1, source_target_pairs={{0,8},{1,57},{2,10},{3,59},{4,12},{5,61},{6,14},{7,63},{8,16},{9,1... | collective-permute-start | bytes 1572872 | tf_op jit(solution)/shard_map/ppermute | solution.py:43
  123.1 20.3 %collective-permute-start.25 = (bf16[96,64,128]{2,1,0:T(8,128)(2,1)S(1)}, bf16[96,64,128]{2,1,0:T(8,128)(2,1)S(1)}, u32[]{:S(2)}, u32[]{:S(2)}) collective-permute-start(bf16[96,64,128]{2,1,0:T(8,128)(2,1)S(1)} %get-tuple-element.33), channel_id=1, source_target_pairs={{0,2},{1,7},{2,4},{3,1},{4,6},{5,3},{6,0},{7,5},{8,10},{9,15},{10,... | collective-permute-start | bytes 4718600 | tf_op jit(solution)/shard_map/ppermute | solution.py:43
  143.4 20.5 %collective-permute-start.26 = (bf16[96,64,128]{2,1,0:T(8,128)(2,1)S(1)}, bf16[96,64,128]{2,1,0:T(8,128)(2,1)S(1)}, u32[]{:S(2)}, u32[]{:S(2)}) collective-permute-start(bf16[96,64,128]{2,1,0:T(8,128)(2,1)S(1)} %collective-permute-done.25), channel_id=1, source_target_pairs={{0,2},{1,7},{2,4},{3,1},{4,6},{5,3},{6,0},{7,5},{8,10},{9,15},{10,... | collective-permute-start | bytes 4718600 | tf_op jit(solution)/shard_map/ppermute | solution.py:43
  163.8 33.5 %collective-permute-start.27 = (bf16[96,64,128]{2,1,0:T(8,128)(2,1)S(1)}, bf16[96,64,128]{2,1,0:T(8,128)(2,1)S(1)}, u32[]{:S(2)}, u32[]{:S(2)}) collective-permute-start(bf16[96,64,128]{2,1,0:T(8,128)(2,1)S(1)} %collective-permute-done.26), channel_id=1, source_target_pairs={{0,2},{1,7},{2,4},{3,1},{4,6},{5,3},{6,0},{7,5},{8,10},{9,15},{10,... | collective-permute-start | bytes 4718600 | tf_op jit(solution)/shard_map/ppermute | solution.py:43
  198.1 7.0 %collective-permute-start.35 = (bf16[24,64,128]{2,1,0:T(8,128)(2,1)S(1)}, bf16[24,64,128]{2,1,0:T(8,128)(2,1)S(1)}, u32[]{:S(2)}, u32[]{:S(2)}) collective-permute-start(bf16[24,64,128]{2,1,0:T(8,128)(2,1)S(1)} %get-tuple-element.64), channel_id=1, source_target_pairs={{0,2},{1,7},{2,4},{3,1},{4,6},{5,3},{6,0},{7,5},{8,10},{9,15},{10,... | collective-permute-start | bytes 1179656 | tf_op jit(solution)/shard_map/ppermute | solution.py:43
  211.8 6.9 %collective-permute-start.37 = (bf16[24,64,128]{2,1,0:T(8,128)(2,1)S(1)}, bf16[24,64,128]{2,1,0:T(8,128)(2,1)S(1)}, u32[]{:S(2)}, u32[]{:S(2)}) collective-permute-start(bf16[24,64,128]{2,1,0:T(8,128)(2,1)S(1)} %collective-permute-done.36), channel_id=1, source_target_pairs={{0,2},{1,7},{2,4},{3,1},{4,6},{5,3},{6,0},{7,5},{8,10},{9,15},{10,... | collective-permute-start | bytes 1179656 | tf_op jit(solution)/shard_map/ppermute | solution.py:43
  218.9 53.8 %collective-permute-start.38 = (bf16[96,64,128]{2,1,0:T(8,128)(2,1)S(1)}, bf16[96,64,128]{2,1,0:T(8,128)(2,1)S(1)}, u32[]{:S(2)}, u32[]{:S(2)}) collective-permute-start(bf16[96,64,128]{2,1,0:T(8,128)(2,1)S(1)} %get-tuple-element.25), channel_id=1, source_target_pairs={{0,64},{1,193},{2,66},{3,195},{4,68},{5,197},{6,70},{7,199},{8,72}... | collective-permute-start | bytes 4718600 | tf_op jit(solution)/shard_map/ppermute | solution.py:43
  239.7 75.0 %collective-permute-start.1 = (bf16[8,8,128,256]{3,2,1,0:T(8,128)(2,1)}, bf16[8,8,128,256]{3,2,1,0:T(8,128)(2,1)}, u32[]{:S(2)}, u32[]{:S(2)}) collective-permute-start(bf16[8,8,128,256]{3,2,1,0:T(8,128)(2,1)} %get-tuple-element.10), channel_id=1, source_target_pairs={{0,1},{1,0},{2,3},{3,2},{4,5},{5,4},{6,7},{7,6},{8,9},{9,8},{10,11... | collective-permute-start | bytes 12582920 | tf_op jit(solution)/shard_map/ppermute | solution.py:310
  272.7 19.6 %collective-permute-start.39 = (bf16[96,64,128]{2,1,0:T(8,128)(2,1)S(1)}, bf16[96,64,128]{2,1,0:T(8,128)(2,1)S(1)}, u32[]{:S(2)}, u32[]{:S(2)}) collective-permute-start(bf16[96,64,128]{2,1,0:T(8,128)(2,1)S(1)} %collective-permute-done.38), channel_id=1, source_target_pairs={{0,64},{1,193},{2,66},{3,195},{4,68},{5,197},{6,70},{7,199},{8,72}... | collective-permute-start | bytes 4718600 | tf_op jit(solution)/shard_map/ppermute | solution.py:43
  292.3 19.7 %collective-permute-start.40 = (bf16[96,64,128]{2,1,0:T(8,128)(2,1)S(1)}, bf16[96,64,128]{2,1,0:T(8,128)(2,1)}, u32[]{:S(2)}, u32[]{:S(2)}) collective-permute-start(bf16[96,64,128]{2,1,0:T(8,128)(2,1)S(1)} %collective-permute-done.39), channel_id=1, source_target_pairs={{0,64},{1,193},{2,66},{3,195},{4,68},{5,197},{6,70},{7,199},{8,72}... | collective-permute-start | bytes 4718600 | tf_op jit(solution)/shard_map/ppermute | solution.py:43
  323.8 6.9 %collective-permute-start.41 = (f32[8,128,128]{2,1,0:T(8,128)S(1)}, f32[8,128,128]{2,1,0:T(8,128)S(1)}, u32[]{:S(2)}, u32[]{:S(2)}) collective-permute-start(f32[8,128,128]{2,1,0:T(8,128)S(1)} %forward_tiles.1.mine_ref), channel_id=1, source_target_pairs={{0,1},{1,0},{2,3},{3,2},{4,5},{5,4},{6,7},{7,6},{8,9},{9,8},{10,11... | collective-permute-start | bytes 1572872 | tf_op jit(solution)/shard_map/ppermute | solution.py:321
  345.4 8.4 %collective-permute-start.42 = (bf16[32,64,128]{2,1,0:T(8,128)(2,1)S(1)}, bf16[32,64,128]{2,1,0:T(8,128)(2,1)S(1)}, u32[]{:S(2)}, u32[]{:S(2)}) collective-permute-start(bf16[32,64,128]{2,1,0:T(8,128)(2,1)S(1)} %slice.195), channel_id=1, source_target_pairs={{0,8},{1,57},{2,10},{3,59},{4,12},{5,61},{6,14},{7,63},{8,16},{9,1... | collective-permute-start | bytes 1572872 | tf_op jit(solution)/shard_map/ppermute | solution.py:61
  355.0 8.4 %collective-permute-start.43 = (bf16[32,64,128]{2,1,0:T(8,128)(2,1)S(1)}, bf16[32,64,128]{2,1,0:T(8,128)(2,1)S(1)}, u32[]{:S(2)}, u32[]{:S(2)}) collective-permute-start(bf16[32,64,128]{2,1,0:T(8,128)(2,1)S(1)} %add_convert_fusion.12), channel_id=1, source_target_pairs={{0,8},{1,57},{2,10},{3,59},{4,12},{5,61},{6,14},{7,63},{8,16},{9,1... | collective-permute-start | bytes 1572872 | tf_op jit(solution)/shard_map/ppermute | solution.py:61
  364.7 8.1 %collective-permute-start.44 = (bf16[32,64,128]{2,1,0:T(8,128)(2,1)S(1)}, bf16[32,64,128]{2,1,0:T(8,128)(2,1)S(1)}, u32[]{:S(2)}, u32[]{:S(2)}) collective-permute-start(bf16[32,64,128]{2,1,0:T(8,128)(2,1)S(1)} %add_convert_fusion.11), channel_id=1, source_target_pairs={{0,8},{1,57},{2,10},{3,59},{4,12},{5,61},{6,14},{7,63},{8,16},{9,1... | collective-permute-start | bytes 1572872 | tf_op jit(solution)/shard_map/ppermute | solution.py:61
  369.2 19.6 %collective-permute-start.55 = (bf16[96,64,128]{2,1,0:T(8,128)(2,1)S(1)}, bf16[96,64,128]{2,1,0:T(8,128)(2,1)S(1)}, u32[]{:S(2)}, u32[]{:S(2)}) collective-permute-start(bf16[96,64,128]{2,1,0:T(8,128)(2,1)S(1)} %get-tuple-element.23), channel_id=1, source_target_pairs={{0,2},{1,7},{2,4},{3,1},{4,6},{5,3},{6,0},{7,5},{8,10},{9,15},{10,... | collective-permute-start | bytes 4718600 | tf_op jit(solution)/shard_map/ppermute | solution.py:61
  369.3 19.6 %collective-permute-start.68 = (bf16[96,64,128]{2,1,0:T(8,128)(2,1)S(1)}, bf16[96,64,128]{2,1,0:T(8,128)(2,1)S(1)}, u32[]{:S(2)}, u32[]{:S(2)}) collective-permute-start(bf16[96,64,128]{2,1,0:T(8,128)(2,1)S(1)} %get-tuple-element.24), channel_id=1, source_target_pairs={{0,64},{1,193},{2,66},{3,195},{4,68},{5,197},{6,70},{7,199},{8,72}... | collective-permute-start | bytes 4718600 | tf_op jit(solution)/shard_map/ppermute | solution.py:61
  374.0 9.2 %collective-permute-start.45 = (bf16[32,64,128]{2,1,0:T(8,128)(2,1)S(1)}, bf16[32,64,128]{2,1,0:T(8,128)(2,1)S(1)}, u32[]{:S(2)}, u32[]{:S(2)}) collective-permute-start(bf16[32,64,128]{2,1,0:T(8,128)(2,1)S(1)} %add_convert_fusion.10), channel_id=1, source_target_pairs={{0,8},{1,57},{2,10},{3,59},{4,12},{5,61},{6,14},{7,63},{8,16},{9,1... | collective-permute-start | bytes 1572872 | tf_op jit(solution)/shard_map/ppermute | solution.py:61
  384.5 9.6 %collective-permute-start.46 = (bf16[32,64,128]{2,1,0:T(8,128)(2,1)S(1)}, bf16[32,64,128]{2,1,0:T(8,128)(2,1)S(1)}, u32[]{:S(2)}, u32[]{:S(2)}) collective-permute-start(bf16[32,64,128]{2,1,0:T(8,128)(2,1)S(1)} %add_convert_fusion.9), channel_id=1, source_target_pairs={{0,8},{1,57},{2,10},{3,59},{4,12},{5,61},{6,14},{7,63},{8,16},{9,1... | collective-permute-start | bytes 1572872 | tf_op jit(solution)/shard_map/ppermute | solution.py:61
  392.3 19.6 %collective-permute-start.56 = (bf16[96,64,128]{2,1,0:T(8,128)(2,1)S(1)}, bf16[96,64,128]{2,1,0:T(8,128)(2,1)S(1)}, u32[]{:S(2)}, u32[]{:S(2)}) collective-permute-start(bf16[96,64,128]{2,1,0:T(8,128)(2,1)S(1)} %get-tuple-element.21), channel_id=1, source_target_pairs={{0,2},{1,7},{2,4},{3,1},{4,6},{5,3},{6,0},{7,5},{8,10},{9,15},{10,... | collective-permute-start | bytes 4718600 | tf_op jit(solution)/shard_map/ppermute | solution.py:61
  393.5 19.6 %collective-permute-start.69 = (bf16[96,64,128]{2,1,0:T(8,128)(2,1)S(1)}, bf16[96,64,128]{2,1,0:T(8,128)(2,1)S(1)}, u32[]{:S(2)}, u32[]{:S(2)}) collective-permute-start(bf16[96,64,128]{2,1,0:T(8,128)(2,1)S(1)} %get-tuple-element.22), channel_id=1, source_target_pairs={{0,64},{1,193},{2,66},{3,195},{4,68},{5,197},{6,70},{7,199},{8,72}... | collective-permute-start | bytes 4718600 | tf_op jit(solution)/shard_map/ppermute | solution.py:61
  395.3 9.3 %collective-permute-start.47 = (bf16[32,64,128]{2,1,0:T(8,128)(2,1)S(1)}, bf16[32,64,128]{2,1,0:T(8,128)(2,1)S(1)}, u32[]{:S(2)}, u32[]{:S(2)}) collective-permute-start(bf16[32,64,128]{2,1,0:T(8,128)(2,1)S(1)} %add_convert_fusion.8), channel_id=1, source_target_pairs={{0,8},{1,57},{2,10},{3,59},{4,12},{5,61},{6,14},{7,63},{8,16},{9,1... | collective-permute-start | bytes 1572872 | tf_op jit(solution)/shard_map/ppermute | solution.py:61
  405.9 12.1 %collective-permute-start.48 = (bf16[32,64,128]{2,1,0:T(8,128)(2,1)S(1)}, bf16[32,64,128]{2,1,0:T(8,128)(2,1)S(1)}, u32[]{:S(2)}, u32[]{:S(2)}) collective-permute-start(bf16[32,64,128]{2,1,0:T(8,128)(2,1)S(1)} %add_convert_fusion.7), channel_id=1, source_target_pairs={{0,8},{1,57},{2,10},{3,59},{4,12},{5,61},{6,14},{7,63},{8,16},{9,1... | collective-permute-start | bytes 1572872 | tf_op jit(solution)/shard_map/ppermute | solution.py:61
  416.4 42.3 %collective-permute-start.57 = (bf16[96,64,128]{2,1,0:T(8,128)(2,1)S(1)}, bf16[96,64,128]{2,1,0:T(8,128)(2,1)S(1)}, u32[]{:S(2)}, u32[]{:S(2)}) collective-permute-start(bf16[96,64,128]{2,1,0:T(8,128)(2,1)S(1)} %get-tuple-element.19), channel_id=1, source_target_pairs={{0,2},{1,7},{2,4},{3,1},{4,6},{5,3},{6,0},{7,5},{8,10},{9,15},{10,... | collective-permute-start | bytes 4718600 | tf_op jit(solution)/shard_map/ppermute | solution.py:61
  417.7 41.0 %collective-permute-start.70 = (bf16[96,64,128]{2,1,0:T(8,128)(2,1)S(1)}, bf16[96,64,128]{2,1,0:T(8,128)(2,1)S(1)}, u32[]{:S(2)}, u32[]{:S(2)}) collective-permute-start(bf16[96,64,128]{2,1,0:T(8,128)(2,1)S(1)} %get-tuple-element.20), channel_id=1, source_target_pairs={{0,64},{1,193},{2,66},{3,195},{4,68},{5,197},{6,70},{7,199},{8,72}... | collective-permute-start | bytes 4718600 | tf_op jit(solution)/shard_map/ppermute | solution.py:61
  419.2 20.4 %collective-permute-start.49 = (bf16[8,64,128]{2,1,0:T(8,128)(2,1)S(1)}, bf16[8,64,128]{2,1,0:T(8,128)(2,1)S(1)}, u32[]{:S(2)}, u32[]{:S(2)}) collective-permute-start(bf16[8,64,128]{2,1,0:T(8,128)(2,1)S(1)} %slice.248), channel_id=1, source_target_pairs={{0,64},{1,193},{2,66},{3,195},{4,68},{5,197},{6,70},{7,199},{8,72}... | collective-permute-start | bytes 393224 | tf_op jit(solution)/shard_map/ppermute | solution.py:61
  419.3 18.1 %collective-permute-start.82 = (f32[128,128]{1,0:T(8,128)S(1)}, f32[128,128]{1,0:T(8,128)S(1)}, u32[]{:S(2)}, u32[]{:S(2)}) collective-permute-start(f32[128,128]{1,0:T(8,128)S(1)} %get-tuple-element.14), channel_id=1, source_target_pairs={{0,2},{2,0},{4,6},{6,4},{8,10},{10,8},{12,14},{14,12},{16,18},{18,... | collective-permute-start | bytes 196616 | tf_op jit(solution)/shard_map/ppermute | solution.py:329
  439.6 7.7 %collective-permute-start.50 = (bf16[8,64,128]{2,1,0:T(8,128)(2,1)S(1)}, bf16[8,64,128]{2,1,0:T(8,128)(2,1)S(1)}, u32[]{:S(2)}, u32[]{:S(2)}) collective-permute-start(bf16[8,64,128]{2,1,0:T(8,128)(2,1)S(1)} %add_convert_fusion.25), channel_id=1, source_target_pairs={{0,64},{1,193},{2,66},{3,195},{4,68},{5,197},{6,70},{7,199},{8,72}... | collective-permute-start | bytes 393224 | tf_op jit(solution)/shard_map/ppermute | solution.py:61
  447.3 11.2 %collective-permute-start.51 = (bf16[8,64,128]{2,1,0:T(8,128)(2,1)S(1)}, bf16[8,64,128]{2,1,0:T(8,128)(2,1)S(1)}, u32[]{:S(2)}, u32[]{:S(2)}) collective-permute-start(bf16[8,64,128]{2,1,0:T(8,128)(2,1)S(1)} %add_convert_fusion.24), channel_id=1, source_target_pairs={{0,64},{1,193},{2,66},{3,195},{4,68},{5,197},{6,70},{7,199},{8,72}... | collective-permute-start | bytes 393224 | tf_op jit(solution)/shard_map/ppermute | solution.py:61
  451.3 7.1 %collective-permute-start.86 = (f32[128,128]{1,0:T(8,128)S(1)}, f32[128,128]{1,0:T(8,128)S(1)}, u32[]{:S(2)}, u32[]{:S(2)}) collective-permute-start(f32[128,128]{1,0:T(8,128)S(1)} %add.379), channel_id=1, source_target_pairs={{0,32},{2,34},{4,36},{6,38},{8,40},{10,42},{12,44},{14,46},{16,48}... | collective-permute-start | bytes 196616 | tf_op jit(solution)/shard_map/ppermute | solution.py:329
  458.4 86.4 %collective-permute-start.87 = (f32[128,128]{1,0:T(8,128)S(1)}, f32[128,128]{1,0:T(8,128)S(1)}, u32[]{:S(2)}, u32[]{:S(2)}) collective-permute-start(f32[128,128]{1,0:T(8,128)S(1)} %add.380), channel_id=1, source_target_pairs={{0,64},{2,66},{4,68},{6,70},{8,72},{10,74},{12,76},{14,78},{16,80}... | collective-permute-start | bytes 196616 | tf_op jit(solution)/shard_map/ppermute | solution.py:329
  458.6 7.7 %collective-permute-start.52 = (bf16[2,64,128]{2,1,0:T(8,128)(2,1)S(1)}, bf16[2,64,128]{2,1,0:T(8,128)(2,1)S(1)}, u32[]{:S(2)}, u32[]{:S(2)}) collective-permute-start(bf16[2,64,128]{2,1,0:T(8,128)(2,1)S(1)} %slice.252), channel_id=1, source_target_pairs={{0,2},{1,7},{2,4},{3,1},{4,6},{5,3},{6,0},{7,5},{8,10},{9,15},{10,... | collective-permute-start | bytes 98312 | tf_op jit(solution)/shard_map/ppermute | solution.py:61
  462.5 8.4 %collective-permute-start.71 = (bf16[24,64,128]{2,1,0:T(8,128)(2,1)S(1)}, bf16[24,64,128]{2,1,0:T(8,128)(2,1)S(1)}, u32[]{:S(2)}, u32[]{:S(2)}) collective-permute-start(bf16[24,64,128]{2,1,0:T(8,128)(2,1)S(1)} %slice.268), channel_id=1, source_target_pairs={{0,2},{1,7},{2,4},{3,1},{4,6},{5,3},{6,0},{7,5},{8,10},{9,15},{10,... | collective-permute-start | bytes 1179656 | tf_op jit(solution)/shard_map/ppermute | solution.py:61
  466.2 8.0 %collective-permute-start.53 = (bf16[2,64,128]{2,1,0:T(8,128)(2,1)S(1)}, bf16[2,64,128]{2,1,0:T(8,128)(2,1)S(1)}, u32[]{:S(2)}, u32[]{:S(2)}) collective-permute-start(bf16[2,64,128]{2,1,0:T(8,128)(2,1)S(1)} %add_convert_fusion.35), channel_id=1, source_target_pairs={{0,2},{1,7},{2,4},{3,1},{4,6},{5,3},{6,0},{7,5},{8,10},{9,15},{10,... | collective-permute-start | bytes 98312 | tf_op jit(solution)/shard_map/ppermute | solution.py:61
  467.0 7.5 %collective-permute-start.59 = (bf16[12,64,128]{2,1,0:T(8,128)(2,1)S(1)}, bf16[12,64,128]{2,1,0:T(8,128)(2,1)S(1)}, u32[]{:S(2)}, u32[]{:S(2)}) collective-permute-start(bf16[12,64,128]{2,1,0:T(8,128)(2,1)S(1)} %add_convert_fusion.22), channel_id=1, source_target_pairs={{0,8},{1,57},{2,10},{3,59},{4,12},{5,61},{6,14},{7,63},{8,16},{9,1... | collective-permute-start | bytes 589832 | tf_op jit(solution)/shard_map/ppermute | solution.py:61
  471.1 7.9 %collective-permute-start.72 = (bf16[24,64,128]{2,1,0:T(8,128)(2,1)S(1)}, bf16[24,64,128]{2,1,0:T(8,128)(2,1)S(1)}, u32[]{:S(2)}, u32[]{:S(2)}) collective-permute-start(bf16[24,64,128]{2,1,0:T(8,128)(2,1)S(1)} %add_convert_fusion.15), channel_id=1, source_target_pairs={{0,2},{1,7},{2,4},{3,1},{4,6},{5,3},{6,0},{7,5},{8,10},{9,15},{10,... | collective-permute-start | bytes 1179656 | tf_op jit(solution)/shard_map/ppermute | solution.py:61
  474.3 8.0 %collective-permute-start.54 = (bf16[2,64,128]{2,1,0:T(8,128)(2,1)S(1)}, bf16[2,64,128]{2,1,0:T(8,128)(2,1)S(1)}, u32[]{:S(2)}, u32[]{:S(2)}) collective-permute-start(bf16[2,64,128]{2,1,0:T(8,128)(2,1)S(1)} %add_convert_fusion.34), channel_id=1, source_target_pairs={{0,2},{1,7},{2,4},{3,1},{4,6},{5,3},{6,0},{7,5},{8,10},{9,15},{10,... | collective-permute-start | bytes 98312 | tf_op jit(solution)/shard_map/ppermute | solution.py:61
  474.6 7.8 %collective-permute-start.60 = (bf16[12,64,128]{2,1,0:T(8,128)(2,1)S(1)}, bf16[12,64,128]{2,1,0:T(8,128)(2,1)S(1)}, u32[]{:S(2)}, u32[]{:S(2)}) collective-permute-start(bf16[12,64,128]{2,1,0:T(8,128)(2,1)S(1)} %add_convert_fusion.21), channel_id=1, source_target_pairs={{0,8},{1,57},{2,10},{3,59},{4,12},{5,61},{6,14},{7,63},{8,16},{9,1... | collective-permute-start | bytes 589832 | tf_op jit(solution)/shard_map/ppermute | solution.py:61
  479.1 7.9 %collective-permute-start.73 = (bf16[24,64,128]{2,1,0:T(8,128)(2,1)S(1)}, bf16[24,64,128]{2,1,0:T(8,128)(2,1)S(1)}, u32[]{:S(2)}, u32[]{:S(2)}) collective-permute-start(bf16[24,64,128]{2,1,0:T(8,128)(2,1)S(1)} %add_convert_fusion.14), channel_id=1, source_target_pairs={{0,2},{1,7},{2,4},{3,1},{4,6},{5,3},{6,0},{7,5},{8,10},{9,15},{10,... | collective-permute-start | bytes 1179656 | tf_op jit(solution)/shard_map/ppermute | solution.py:61
  518.5 34.1 %collective-permute-start.81 = (f32[8,64,128]{2,1,0:T(8,128)S(1)}, f32[8,64,128]{2,1,0:T(8,128)S(1)}, u32[]{:S(2)}, u32[]{:S(2)}) collective-permute-start(f32[8,64,128]{2,1,0:T(8,128)S(1)} %get-tuple-element.32), channel_id=1, source_target_pairs={{0,1},{1,0},{2,3},{3,2},{4,5},{5,4},{6,7},{7,6},{8,9},{9,8},{10,11... | collective-permute-start | bytes 786440 | tf_op jit(solution)/shard_map/ppermute | solution.py:337
  (50 other events, 389.6 us)
